TPU v7x, 32 devices: a whole 2x2x4 slice. The times are simulated.
32 devices in a mesh: grp: 2 (over core), ctx: 16 (over z, y, x).
Axes of the slice: x: 2, y: 2, z: 4, core: 2. Of those that a mesh axis runs over, the one named last changes fastest.
Arguments:
- queries: bfloat16 [4096, 4096], P(('grp', 'ctx')), may hold values from -6 to 6
- keys: bfloat16 [4096, 512], P(('grp', 'ctx')), may hold values from -6 to 6
- values: bfloat16 [4096, 512], P(('grp', 'ctx')), may hold values from -6 to 6
- d_unit: bfloat16 [4096, 4096], P(('grp', 'ctx')), may hold values from -6 to 6
- token_terms: float32 [4096], P(('grp', 'ctx')), may hold values from -4 to 4
- spans: int32 [8, 3], P('grp'), may hold values from 1 to 3, as said below
Outputs:
- attended: bfloat16 [4096, 4096], P(('grp', 'ctx'))
- query_grad: bfloat16 [4096, 4096], P(('grp', 'ctx'))
- key_gradient: bfloat16 [4096, 512], P(('grp', 'ctx'))
- value_gradient: bfloat16 [4096, 512], P(('grp', 'ctx'))
Inputs may be any that keep to these rules, and one draw needn't show every extreme that they name: `spans`: each row's 4 examples have 3 to 5 tiles each and fill its 16 tiles exactly; every span has at least one tile; every row has an example of exactly 5 tiles.
All inputs are finite; a program needn't handle non-finite values.
Results may differ from a plain program's by a relative error of at most 0.012.
The roundings to bfloat16 on the way count: a program that leaves them out, or rounds other values in their place, can miss the bound.
Values may be sent and summed in bfloat16 or wider, within the bound.
A program may use at most 128 MiB of HBM per device.

v0:
```python
from functools import partial

import jax
import jax.numpy as jnp
from jax import lax
from jax.sharding import PartitionSpec as P

QUERY_HEADS = 32
KEY_VALUE_HEADS = 4
HEAD_SIZE = 128
MAX_TILES = 5


preference_beta = 0.3


def from_behind(shard, axis, by):
    length = lax.axis_size(axis)
    pairs = [(i, i + by) for i in range(length) if 0 <= i + by < length]
    return lax.ppermute(shard, axis, pairs)


def tile_meta(spans_row, tile_index):
    counts = spans_row[:, 0] + spans_row[:, 1] + spans_row[:, 2]
    ends = jnp.cumsum(counts)
    starts = ends - counts
    example = jnp.sum((starts[None, :] <= tile_index[:, None]).astype(jnp.int32), axis=1) - 1
    labels = jnp.arange(spans_row.shape[0], dtype=jnp.int32)
    hits = (example[:, None] == labels[None, :]).astype(jnp.int32)
    within = tile_index - jnp.sum(hits * starts[None, :], axis=1)
    prompt = jnp.sum(hits * spans_row[None, :, 0], axis=1)
    chosen = jnp.sum(hits * spans_row[None, :, 1], axis=1)
    kind = jnp.where(within < prompt, 0, jnp.where(within < prompt + chosen, 1, 2)).astype(
        jnp.int32
    )
    return (example, kind, hits)


def per_device(queries, keys, values, d_unit, token_terms, spans):
    rows_per_tile = queries.shape[0]
    heads_per_group = QUERY_HEADS // KEY_VALUE_HEADS
    score_scale = HEAD_SIZE ** (-0.5)
    position = lax.axis_index("ctx")
    key_tiles = position - jnp.arange(MAX_TILES, dtype=jnp.int32)
    key_example, key_kind, unused_hits = tile_meta(spans, key_tiles)
    own_example, own_kind, own_hits = tile_meta(spans, jnp.reshape(position, (1,)))
    blocked = (own_kind[0] == 2) & (key_kind == 1)
    live_tiles = (key_tiles >= 0) & (key_example == own_example[0]) & jnp.logical_not(blocked)
    polarity = jnp.where(own_kind[0] == 1, 1.0, jnp.where(own_kind[0] == 2, -1.0, 0.0)).astype(
        jnp.float32
    )
    own_margin = polarity * jnp.sum(token_terms)
    member = own_hits[0].astype(jnp.float32)
    margins = lax.psum(member * own_margin, "ctx")
    batch_sum = lax.psum(jnp.sum(margins), "grp")
    center = batch_sum / (spans.shape[0] * lax.axis_size("grp"))
    weights = jax.nn.sigmoid(preference_beta * (center - margins))
    own_weight = jnp.sum(member * weights)
    key_value = jnp.stack([keys, values])
    span_window = key_value[None]
    reached = 1
    while reached < MAX_TILES:
        needed = min(reached, MAX_TILES - reached)
        arrived = from_behind(span_window[:needed], "ctx", reached)
        span_window = jnp.concatenate([span_window, arrived], axis=0)
        reached = reached + needed
    query_heads = queries.reshape(rows_per_tile, KEY_VALUE_HEADS, heads_per_group, HEAD_SIZE)
    causal = jnp.arange(rows_per_tile)[:, None] >= jnp.arange(rows_per_tile)[None, :]
    stat_dims = (KEY_VALUE_HEADS, heads_per_group, rows_per_tile, 1)
    output_dims = (rows_per_tile, KEY_VALUE_HEADS, heads_per_group, HEAD_SIZE)

    def key_block(start_shift):
        return span_window[start_shift, 0].reshape(rows_per_tile, KEY_VALUE_HEADS, HEAD_SIZE)

    def value_block(start_shift):
        return span_window[start_shift, 1].reshape(rows_per_tile, KEY_VALUE_HEADS, HEAD_SIZE)

    def masked_scores(start_shift):
        raw = (
            jnp.einsum(
                "ihgc,jhc->hgij",
                query_heads,
                key_block(start_shift),
                preferred_element_type=jnp.float32,
            )
            * score_scale
        )
        if start_shift == 0:
            raw = jnp.where(causal, raw, -jnp.inf)
        return raw

    def block_stats(start_shift):
        score_block = masked_scores(start_shift)
        block_max = jnp.max(score_block, axis=-1, keepdims=True)
        block_total = jnp.sum(jnp.exp(score_block - block_max), axis=-1, keepdims=True)
        return (block_max, block_total)

    def empty_stats():
        return (jnp.full(stat_dims, -jnp.inf, jnp.float32), jnp.zeros(stat_dims, jnp.float32))

    stats = [block_stats(0)]
    for start_shift in range(1, MAX_TILES):
        stats.append(
            lax.cond(live_tiles[start_shift], partial(block_stats, start_shift), empty_stats)
        )
    row_max = stats[0][0]
    for pair_stats in stats[1:]:
        row_max = jnp.maximum(row_max, pair_stats[0])
    exp_total = jnp.zeros_like(row_max)
    for pair_stats in stats:
        exp_total = exp_total + pair_stats[1] * jnp.exp(pair_stats[0] - row_max)
    lse = row_max + jnp.log(exp_total)

    def forward_block(start_shift):
        rounded = jnp.exp(masked_scores(start_shift) - lse).astype(jnp.bfloat16)
        return jnp.einsum(
            "hgij,jhc->ihgc", rounded, value_block(start_shift), preferred_element_type=jnp.float32
        )

    def empty_output():
        return jnp.zeros(output_dims, jnp.float32)

    output_sum = forward_block(0)
    for start_shift in range(1, MAX_TILES):
        output_sum = output_sum + lax.cond(
            live_tiles[start_shift], partial(forward_block, start_shift), empty_output
        )
    attended = output_sum.astype(jnp.bfloat16).reshape(rows_per_tile, QUERY_HEADS * HEAD_SIZE)
    output_gradient = (own_weight * d_unit.astype(jnp.float32)).astype(jnp.bfloat16)
    group_heads = output_gradient.reshape(
        rows_per_tile, KEY_VALUE_HEADS, heads_per_group, HEAD_SIZE
    )
    row_dots = jnp.transpose(
        jnp.sum(group_heads.astype(jnp.float32) * output_sum, axis=-1), (1, 2, 0)
    )[..., None]

    def backward_block(start_shift):
        probability = jnp.exp(masked_scores(start_shift) - lse)
        rounded = probability.astype(jnp.bfloat16)
        dprob = jnp.einsum(
            "ihgc,jhc->hgij",
            group_heads,
            value_block(start_shift),
            preferred_element_type=jnp.float32,
        )
        dscores = (probability * (dprob - row_dots) * score_scale).astype(jnp.bfloat16)
        query_part = jnp.einsum(
            "hgij,jhc->ihgc", dscores, key_block(start_shift), preferred_element_type=jnp.float32
        )
        key_portion = jnp.einsum(
            "hgij,ihgc->jhc", dscores, query_heads, preferred_element_type=jnp.float32
        )
        value_portion = jnp.einsum(
            "hgij,ihgc->jhc", rounded, group_heads, preferred_element_type=jnp.float32
        )
        return (
            query_part,
            jnp.stack(
                [
                    key_portion.reshape(rows_per_tile, KEY_VALUE_HEADS * HEAD_SIZE),
                    value_portion.reshape(rows_per_tile, KEY_VALUE_HEADS * HEAD_SIZE),
                ]
            ),
        )

    def empty_backward():
        return (
            jnp.zeros(output_dims, jnp.float32),
            jnp.zeros((2, rows_per_tile, KEY_VALUE_HEADS * HEAD_SIZE), jnp.float32),
        )

    query_sum, first_part = backward_block(0)
    contributions = [first_part]
    for start_shift in range(1, MAX_TILES):
        query_part, pair_part = lax.cond(
            live_tiles[start_shift], partial(backward_block, start_shift), empty_backward
        )
        query_sum = query_sum + query_part
        contributions.append(pair_part)
    contributions = jnp.stack(contributions)
    buffer = contributions
    length = MAX_TILES
    while length > 1:
        distance = 1 << (length - 1).bit_length() - 1
        arrived = from_behind(buffer[distance:length], "ctx", -distance)
        buffer = jnp.concatenate(
            [buffer[: length - distance] + arrived, buffer[length - distance : distance]], axis=0
        )
        length = distance
    own_grads = buffer[0]
    query_grad = query_sum.astype(jnp.bfloat16).reshape(rows_per_tile, QUERY_HEADS * HEAD_SIZE)
    key_gradient = own_grads[0].astype(jnp.bfloat16)
    value_gradient = own_grads[1].astype(jnp.bfloat16)
    return (attended, query_grad, key_gradient, value_gradient)


def solution(mesh):
    return jax.shard_map(
        per_device,
        mesh=mesh,
        in_specs=(
            P(("grp", "ctx"), None),
            P(("grp", "ctx"), None),
            P(("grp", "ctx"), None),
            P(("grp", "ctx"), None),
            P(("grp", "ctx")),
            P("grp", None),
        ),
        out_specs=(
            P(("grp", "ctx"), None),
            P(("grp", "ctx"), None),
            P(("grp", "ctx"), None),
            P(("grp", "ctx"), None),
        ),
        check_vma=False,
    )
```

profile of v0, /device:TPU:18, one launch (start us, length us, event | category | flops | bytes accessed | tf_op | source)
XLA Modules:
  0.0 191.9 jit_solution(5991633423217396498)
XLA Ops:
  0.7 1.2 copy.269
  1.8 1.0 copy.270
  3.6 3.4 %collective-permute-start = (bf16[1,2,128,512]{2,3,1,0:T(8,128)(2,1)}, bf16[1,2,128,512]{2,3,1,0:T(8,128)(2,1)S(1)}, u32[]{:S(2)}, u32[]{:S(2)}) collective-permute-start(bf16[1,2,128,512]{2,3,1,0:T(8,128)(2,1)} %maximum_bitcast_fusion.4), channel_id=1, source_target_pairs={{0,1},{1,2},{2,3},{3,4},{4,5},{5,6},{6,7},{7,8},{8,9},{9,10},{10,1... | collective-permute-start | bytes 786440 | tf_op jit(solution)/shard_map/ppermute | solution.py:20
  7.0 3.5 %collective-permute-start.2 = (bf16[1,2,128,512]{2,3,1,0:T(8,128)(2,1)}, bf16[1,2,128,512]{2,3,1,0:T(8,128)(2,1)}, u32[]{:S(2)}, u32[]{:S(2)}) collective-permute-start(bf16[1,2,128,512]{2,3,1,0:T(8,128)(2,1)} %maximum_bitcast_fusion.4), channel_id=1, source_target_pairs={{0,4},{1,5},{2,6},{3,7},{4,8},{5,9},{6,10},{7,11},{8,12},{9,13},{1... | collective-permute-start | bytes 786440 | tf_op jit(solution)/shard_map/ppermute | solution.py:20
  10.5 1.0 slice_reduce_fusion.2
  12.3 1.6 fusion.115
  20.3 1.3 reduce_sum.168
  22.4 29.9 %psum.14 = f32[4]{0:T(128)S(1)} all-reduce(f32[4]{0:T(128)S(1)} %fusion.103), channel_id=1, replica_groups=mesh['grp'=2,'ctx'=16] {'ctx'}, use_global_device_ids=true, to_apply=%region_36.37 | all-reduce | flops 4 | bytes 32 | tf_op jit(solution)/shard_map/psum | solution.py:54
  53.5 3.1 %psum.15 = f32[]{:T(128)} all-reduce(f32[]{:T(128)} %reduce_sum.169), channel_id=1, replica_groups=mesh['grp'=2,'ctx'=16] {'grp'}, use_global_device_ids=true, to_apply=%region_38.39 | all-reduce | flops 1 | bytes 8 | tf_op jit(solution)/shard_map/psum | solution.py:55
  58.8 2.6 %fusion.117 = (f32[4,8,128]{2,1,0:T(8,128)S(1)}, f32[4,8,128,128]{2,3,1,0:T(8,128)}) fusion(bf16[128,4,128,1]{0,2,3,1:T(8,128)(2,1)S(1)} %bitcast.572, bf16[128,4,8,128]{0,3,2,1:T(8,128)(2,1)S(1)} %bitcast.535, pred[128,128]{0,1:T(8,128)(4,1)} %iota_compare_fusion), kind=kOutput, calls=%fused_computation.185 | convolution fusion | flops 135786496 | bytes 3309568 | tf_op jit(solution)/shard_map/ihgc,jhc->hgij/dot_general | solution.py:80
  61.4 1.8 pad_maximum_fusion.2
  63.2 2.1 %collective-permute-start.1 = (bf16[2,2,128,512]{2,3,1,0:T(8,128)(2,1)}, bf16[2,2,128,512]{2,3,1,0:T(8,128)(2,1)}, u32[]{:S(2)}, u32[]{:S(2)}) collective-permute-start(bf16[2,2,128,512]{2,3,1,0:T(8,128)(2,1)} %pad_maximum_fusion.2), channel_id=1, source_target_pairs={{0,2},{1,3},{2,4},{3,5},{4,6},{5,7},{6,8},{7,9},{8,10},{9,11},{10,... | collective-permute-start | bytes 1572872 | tf_op jit(solution)/shard_map/ppermute | solution.py:20
  69.1 1.9 %exponential_reduce_fusion = f32[4,8,128]{2,1,0:T(8,128)S(1)} fusion(f32[4,8,128,128]{2,3,1,0:T(8,128)} %get-tuple-element.322, f32[4,8,128]{2,1,0:T(8,128)S(1)} %get-tuple-element.321), kind=kLoop, calls=%fused_computation.113 | loop fusion | flops 1044480 | bytes 2129920 | tf_op jit(solution)/shard_map/reduce_sum | solution.py:95
  72.3 8.0 %collective-permute-done.1 = bf16[2,2,128,512]{2,3,1,0:T(8,128)(2,1)} collective-permute-done((bf16[2,2,128,512]{2,3,1,0:T(8,128)(2,1)}, bf16[2,2,128,512]{2,3,1,0:T(8,128)(2,1)}, u32[]{:S(2)}, u32[]{:S(2)}) %collective-permute-start.1) | collective-permute-done | bytes 524320 | tf_op jit(solution)/shard_map/ppermute | solution.py:20
  80.3 3.1 %conditional.13 = (f32[4,8,128,1]{2,1,0,3:T(8,128)}, f32[4,8,128,1]{2,1,0,3:T(8,128)S(1)}) conditional(s32[]{:T(128)} %bitcast.139, () %tuple.104, (bf16[2,2,128,512]{2,3,1,0:T(8,128)(2,1)}, bf16[128,4,8,128]{0,3,2,1:T(8,128)(2,1)S(1)}) %tuple.235), branch_computations={%region_14.15_spmd, %region_15.18_spmd} | conditional | flops 136830976 | bytes 5685264 | solution.py:104
  81.2 1.1 bitcast_reduce_fusion.1
  82.3 1.1 fusion.3
  83.4 3.2 %conditional.14 = (f32[4,8,128,1]{2,1,0,3:T(8,128)}, f32[4,8,128,1]{2,1,0,3:T(8,128)S(1)}) conditional(s32[]{:T(128)} %bitcast.140, () %tuple.106, (bf16[2,2,128,512]{2,3,1,0:T(8,128)(2,1)}, bf16[128,4,8,128]{0,3,2,1:T(8,128)(2,1)S(1)}) %tuple.236), branch_computations={%region_18.19_spmd, %region_19.22_spmd} | conditional | flops 136830976 | bytes 5685264 | solution.py:104
  84.4 1.1 bitcast_reduce_fusion.2
  85.5 1.1 fusion.5
  87.4 6.1 %conditional.17 = (f32[128,4,8,128]{0,3,2,1:T(8,128)}) conditional(s32[]{:T(128)} %bitcast.139, () %tuple.111, (bf16[2,2,128,512]{2,3,1,0:T(8,128)(2,1)}, bf16[128,4,8,128]{0,3,2,1:T(8,128)(2,1)S(1)}, f32[4,8,128,1]{2,1,0,3:T(8,128)S(1)}) %tuple.237), branch_computations={%region_29.30_spmd, %region_30.31_spmd} | conditional | flops 270008320 | bytes 8142856 | solution.py:125
  88.4 2.2 %convolution_bitcast_fusion.1 = f32[128,4,8,128]{3,0,2,1:T(8,128)} fusion(bf16[128,4,128,1]{0,2,3,1:T(8,128)(2,1)S(1)} %bitcast.615, bf16[128,4,128,1]{0,2,3,1:T(8,128)(2,1)S(1)} %bitcast.614, bf16[128,4,8,128]{0,3,2,1:T(8,128)(2,1)S(1)} %get-tuple-element.255, f32[4,8,128]{2,1,0:T(8,128)S(1)} %bitcast.558), kind=kOutput, calls=%fused_computation.26 | convolution fusion | flops 270008320 | bytes 3424256 | tf_op jit(solution)/shard_map/cond/branch_1_fun/hgij,jhc->ihgc/dot_general | solution.py:116
  90.6 3.0 %copy.436 = f32[128,4,8,128]{0,3,2,1:T(8,128)} copy(f32[128,4,8,128]{3,0,2,1:T(8,128)} %convolution_bitcast_fusion.1) | data formatting | bytes 4194304 | tf_op jit(solution)/shard_map/cond | solution.py:125
  93.6 6.1 %conditional.18 = (f32[128,4,8,128]{0,3,2,1:T(8,128)}) conditional(s32[]{:T(128)} %bitcast.140, () %tuple.113, (bf16[2,2,128,512]{2,3,1,0:T(8,128)(2,1)}, bf16[128,4,8,128]{0,3,2,1:T(8,128)(2,1)S(1)}, f32[4,8,128,1]{2,1,0,3:T(8,128)S(1)}) %tuple.238), branch_computations={%region_31.32_spmd, %region_32.33_spmd} | conditional | flops 270008320 | bytes 8142856 | solution.py:125
  93.6 1.0 fusion.109
  94.6 2.2 %convolution_bitcast_fusion.2 = f32[128,4,8,128]{3,0,2,1:T(8,128)} fusion(bf16[128,4,128,1]{0,2,3,1:T(8,128)(2,1)S(1)} %bitcast.617, bf16[128,4,128,1]{0,2,3,1:T(8,128)(2,1)S(1)} %bitcast.616, bf16[128,4,8,128]{0,3,2,1:T(8,128)(2,1)S(1)} %get-tuple-element.258, f32[4,8,128]{2,1,0:T(8,128)S(1)} %bitcast.559), kind=kOutput, calls=%fused_computation.33 | convolution fusion | flops 270008320 | bytes 3424256 | tf_op jit(solution)/shard_map/cond/branch_1_fun/hgij,jhc->ihgc/dot_general | solution.py:116
  96.8 2.9 %copy.438 = f32[128,4,8,128]{0,3,2,1:T(8,128)} copy(f32[128,4,8,128]{3,0,2,1:T(8,128)} %convolution_bitcast_fusion.2) | data formatting | bytes 4194304 | tf_op jit(solution)/shard_map/cond | solution.py:125
  99.7 3.3 %fusion.83 = f32[4,128,8,128]{3,1,2,0:T(8,128)} fusion(bf16[128,4,128,1]{0,2,3,1:T(8,128)(2,1)S(1)} %bitcast.575, f32[4,8,128,128]{2,3,1,0:T(8,128)} %get-tuple-element.322, f32[4,8,128]{2,1,0:T(8,128)S(1)} %bitcast.555), kind=kOutput, calls=%fused_computation.123 | convolution fusion | flops 135266304 | bytes 4341760 | tf_op jit(solution)/shard_map/hgij,jhc->ihgc/dot_general | solution.py:116
  103.0 1.6 conditional.16
  103.0 1.6 broadcast.198.clone
  104.6 1.6 conditional.19
  104.6 1.6 broadcast.204.clone
  106.2 6.4 %multiply_reduce_fusion = (f32[128,4,8]{0,2,1:T(8,128)S(1)}, bf16[128,4,8,128]{0,3,2,1:T(8,128)(2,1)}) fusion(bf16[128,4096]{0,1:T(8,128)(2,1)S(1)} %copy.287, f32[128,4,8,128]{0,3,2,1:T(8,128)} %get-tuple-element.270, f32[128,4,8,128]{0,3,2,1:T(8,128)} %get-tuple-element.269, f32[128,4,8,128]{0,3,2,1:T(8,128)} %get-tuple-element.268, ...), kind=kLoop, calls=%fused_computation.110 | loop fusion | flops 4190208 | bytes 12599296 | tf_op jit(solution)/shard_map/reduce_sum | solution.py:134
  112.6 1.7 conditional.23
  112.6 1.6 broadcast.215.clone
  115.2 1.9 collective-permute-start.3
  117.2 12.7 %conditional.21 = (f32[128,4,8,128]{0,3,2,1:T(8,128)}, f32[1,2,128,512]{3,2,1,0:T(8,128)}) conditional(s32[]{:T(128)} %bitcast.139, () %tuple.118, (bf16[2,2,128,512]{2,3,1,0:T(8,128)(2,1)}, bf16[128,4,8,128]{0,3,2,1:T(8,128)(2,1)S(1)}, f32[4,8,128,1]{2,1,0,3:T(8,128)S(1)}, bf16[128,4,8,128]{0,3,2,1:T(8,128)(2,1)S(1)}, ...), branch_computations={%region_43.44_spmd, %region_44.45_spmd} | conditional | flops 675938304 | bytes 24100936 | solution.py:175
  118.9 1.5 fusion.40
  122.2 2.1 %copy.448 = f32[1,2,128,512]{3,2,1,0:T(8,128)} copy(f32[1,2,128,512]{2,3,1,0:T(8,128)} %maximum_bitcast_fusion.1) | data formatting | bytes 1048576 | tf_op jit(solution)/shard_map/cond | solution.py:175
  124.2 2.8 %convolution_bitcast_fusion.5 = f32[128,4,8,128]{3,0,2,1:T(8,128)} fusion(bf16[4,8,128,128]{2,3,1,0:T(8,128)(2,1)S(1)} %fusion.40, bf16[128,4,128,1]{0,2,3,1:T(8,128)(2,1)} %bitcast.577), kind=kOutput, calls=%fused_computation.64 | convolution fusion | flops 134217728 | bytes 3276800 | tf_op jit(solution)/shard_map/cond/branch_1_fun/hgij,jhc->ihgc/dot_general | solution.py:147
  127.0 2.9 %copy.446 = f32[128,4,8,128]{0,3,2,1:T(8,128)} copy(f32[128,4,8,128]{3,0,2,1:T(8,128)} %convolution_bitcast_fusion.5) | data formatting | bytes 4194304 | tf_op jit(solution)/shard_map/cond | solution.py:175
  129.9 12.1 %conditional.22 = (f32[128,4,8,128]{0,3,2,1:T(8,128)}, f32[1,2,128,512]{3,2,1,0:T(8,128)S(1)}) conditional(s32[]{:T(128)} %bitcast.140, () %tuple.120, (bf16[2,2,128,512]{2,3,1,0:T(8,128)(2,1)}, bf16[128,4,8,128]{0,3,2,1:T(8,128)(2,1)S(1)}, f32[4,8,128,1]{2,1,0,3:T(8,128)S(1)}, bf16[128,4,8,128]{0,3,2,1:T(8,128)(2,1)S(1)}, ...), branch_computations={%region_45.46_spmd, %region_46.47_spmd} | conditional | flops 675938304 | bytes 26198116 | solution.py:175
  129.9 1.0 fusion.113
  134.1 2.1 %copy.452 = f32[1,2,128,512]{3,2,1,0:T(8,128)} copy(f32[1,2,128,512]{2,3,1,0:T(8,128)} %maximum_bitcast_fusion.2) | data formatting | bytes 1048576 | tf_op jit(solution)/shard_map/cond | solution.py:175
  136.2 2.8 %convolution_bitcast_fusion.6 = f32[128,4,8,128]{3,0,2,1:T(8,128)} fusion(bf16[4,8,128,128]{2,3,1,0:T(8,128)(2,1)S(1)} %fusion.50, bf16[128,4,128,1]{0,2,3,1:T(8,128)(2,1)} %bitcast.579), kind=kOutput, calls=%fused_computation.77 | convolution fusion | flops 134217728 | bytes 3276800 | tf_op jit(solution)/shard_map/cond/branch_1_fun/hgij,jhc->ihgc/dot_general | solution.py:147
  139.0 3.0 %copy.450 = f32[128,4,8,128]{0,3,2,1:T(8,128)} copy(f32[128,4,8,128]{3,0,2,1:T(8,128)} %convolution_bitcast_fusion.6) | data formatting | bytes 4194304 | tf_op jit(solution)/shard_map/cond | solution.py:175
  141.9 2.2 %pad_maximum_fusion.1 = f32[2,2,128,512]{3,2,1,0:T(8,128)} fusion(f32[1,2,128,512]{3,2,1,0:T(8,128)S(1)} %get-tuple-element.276, f32[1,2,128,512]{3,2,1,0:T(8,128)} %get-tuple-element.274), kind=kLoop, calls=%fused_computation.116 | loop fusion | flops 262144 | bytes 2097152 | tf_op jit(solution)/shard_map/stack | solution.py:180
  144.2 2.1 %collective-permute-start.4 = (f32[2,2,128,512]{3,2,1,0:T(8,128)}, f32[2,2,128,512]{3,2,1,0:T(8,128)}, u32[]{:S(2)}, u32[]{:S(2)}) collective-permute-start(f32[2,2,128,512]{3,2,1,0:T(8,128)} %pad_maximum_fusion.1), channel_id=1, source_target_pairs={{2,0},{3,1},{4,2},{5,3},{6,4},{7,5},{8,6},{9,7},{10,8},{11,9},{12,... | collective-permute-start | bytes 3145736 | tf_op jit(solution)/shard_map/ppermute | solution.py:20
  146.3 1.6 fusion.74
  147.9 1.1 fusion.127
  149.1 1.8 copy.297
  150.9 2.8 %fusion.81 = f32[4,128,128,1]{2,1,3,0:T(8,128)} fusion(bf16[128,4,8,128]{0,3,2,1:T(8,128)(2,1)S(1)} %bitcast.553, f32[4,8,128,128]{2,3,1,0:T(8,128)} %get-tuple-element.322, f32[4,8,128]{2,1,0:T(8,128)S(1)} %bitcast.557), kind=kOutput, calls=%fused_computation.122 | convolution fusion | flops 135266304 | bytes 3424256 | tf_op jit(solution)/shard_map/hgij,ihgc->jhc/dot_general | solution.py:153
  153.6 1.8 copy.298
  155.4 2.5 %conditional.20 = (f32[128,4,8,128]{0,3,2,1:T(8,128)}, f32[1,2,128,512]{3,2,1,0:T(8,128)}) conditional(s32[]{:T(128)} %bitcast.138, () %tuple.116, (bf16[1,2,128,512]{2,3,1,0:T(8,128)(2,1)S(1)}, bf16[128,4,8,128]{0,3,2,1:T(8,128)(2,1)S(1)}, f32[4,8,128,1]{2,1,0,3:T(8,128)S(1)}, bf16[128,4,8,128]{0,3,2,1:T(8,128)(2,1)S(1)}, ...), branch_computations={%region_41.42_spmd, %region_42.43_spmd} | conditional | flops 675938304 | bytes 33013916 | solution.py:175
  155.4 1.6 broadcast.206.clone
  157.9 1.3 fusion.80
  159.2 11.3 %collective-permute-done.4 = f32[2,2,128,512]{3,2,1,0:T(8,128)} collective-permute-done((f32[2,2,128,512]{3,2,1,0:T(8,128)}, f32[2,2,128,512]{3,2,1,0:T(8,128)}, u32[]{:S(2)}, u32[]{:S(2)}) %collective-permute-start.4) | collective-permute-done | bytes 1048608 | tf_op jit(solution)/shard_map/ppermute | solution.py:20
  170.5 1.6 maximum_add_fusion
  172.9 1.9 collective-permute-start.5
  175.3 4.6 %fusion.71 = bf16[128,4,8,128]{0,3,2,1:T(8,128)(2,1)S(1)} fusion(f32[128,4,8,128]{0,3,2,1:T(8,128)} %get-tuple-element.277, f32[128,4,8,128]{0,3,2,1:T(8,128)} %get-tuple-element.275, f32[128,4,8,128]{0,3,2,1:T(8,128)} %get-tuple-element.273, f32[128,4,8,128]{0,3,2,1:T(8,128)} %get-tuple-element.271, f32[4,128,8,128]{3,1,2,0:T(8,128)S(1)} %fusion.126), kind=kLoop, calls=%fused_computation.100 | loop fusion | flops 2621440 | bytes 11534336 | tf_op jit(solution)/shard_map/convert_element_type | solution.py:191
  179.8 1.3 copy.304
  181.1 1.3 copy.303
  182.4 7.7 %collective-permute-done.5 = f32[1,2,128,512]{3,2,1,0:T(8,128)} collective-permute-done((f32[1,2,128,512]{3,2,1,0:T(8,128)}, f32[1,2,128,512]{3,2,1,0:T(8,128)}, u32[]{:S(2)}, u32[]{:S(2)}) %collective-permute-start.5) | collective-permute-done | bytes 524320 | tf_op jit(solution)/shard_map/ppermute | solution.py:20
  190.1 1.1 fusion.79
  (85 shorter events, 25.5 us)
Async XLA Ops:
  0.6 52.2 %copy-start.11 = (bf16[128,4096]{1,0:T(8,128)(2,1)S(1)}, bf16[128,4096]{1,0:T(8,128)(2,1)}, u32[]{:S(2)}) copy-start(bf16[128,4096]{1,0:T(8,128)(2,1)} %param.30) | copy-start | bytes 3145732
  0.6 57.3 %copy-start.10 = (bf16[128,4096]{1,0:T(8,128)(2,1)S(1)}, bf16[128,4096]{1,0:T(8,128)(2,1)}, u32[]{:S(2)}) copy-start(bf16[128,4096]{1,0:T(8,128)(2,1)} %param.33) | copy-start | bytes 3145732
  3.6 57.8 %collective-permute-start = (bf16[1,2,128,512]{2,3,1,0:T(8,128)(2,1)}, bf16[1,2,128,512]{2,3,1,0:T(8,128)(2,1)S(1)}, u32[]{:S(2)}, u32[]{:S(2)}) collective-permute-start(bf16[1,2,128,512]{2,3,1,0:T(8,128)(2,1)} %maximum_bitcast_fusion.4), channel_id=1, source_target_pairs={{0,1},{1,2},{2,3},{3,4},{4,5},{5,6},{6,7},{7,8},{8,9},{9,10},{10,1... | collective-permute-start | bytes 786440 | tf_op jit(solution)/shard_map/ppermute | solution.py:20
  7.0 64.7 %collective-permute-start.2 = (bf16[1,2,128,512]{2,3,1,0:T(8,128)(2,1)}, bf16[1,2,128,512]{2,3,1,0:T(8,128)(2,1)}, u32[]{:S(2)}, u32[]{:S(2)}) collective-permute-start(bf16[1,2,128,512]{2,3,1,0:T(8,128)(2,1)} %maximum_bitcast_fusion.4), channel_id=1, source_target_pairs={{0,4},{1,5},{2,6},{3,7},{4,8},{5,9},{6,10},{7,11},{8,12},{9,13},{1... | collective-permute-start | bytes 786440 | tf_op jit(solution)/shard_map/ppermute | solution.py:20
  19.1 0.5 copy-start.21
  58.8 6.5 %copy-start.18 = (s32[5]{0:T(128)S(1)}, s32[5]{0:T(128)}, u32[]{:S(2)}) copy-start(s32[5]{0:T(128)} %get-tuple-element.281) | copy-start | bytes 64
  58.8 6.5 %copy-start.19 = (s32[5]{0:T(128)S(1)}, s32[5]{0:T(128)}, u32[]{:S(2)}) copy-start(s32[5]{0:T(128)} %get-tuple-element.282) | copy-start | bytes 64
  58.8 6.5 %copy-start.20 = (s32[5]{0:T(128)S(1)}, s32[5]{0:T(128)}, u32[]{:S(2)}) copy-start(s32[5]{0:T(128)} %get-tuple-element.283) | copy-start | bytes 64
  58.8 6.5 %copy-start.22 = (s32[5]{0:T(128)S(1)}, s32[5]{0:T(128)}, u32[]{:S(2)}) copy-start(s32[5]{0:T(128)} %copy-done.21) | copy-start | bytes 64
  61.4 9.7 %copy-start.16 = (f32[4,8,128]{2,1,0:T(8,128)}, f32[4,8,128]{2,1,0:T(8,128)S(1)}, u32[]{:S(2)}) copy-start(f32[4,8,128]{2,1,0:T(8,128)S(1)} %get-tuple-element.321) | copy-start | bytes 49156
  63.2 17.1 %collective-permute-start.1 = (bf16[2,2,128,512]{2,3,1,0:T(8,128)(2,1)}, bf16[2,2,128,512]{2,3,1,0:T(8,128)(2,1)}, u32[]{:S(2)}, u32[]{:S(2)}) collective-permute-start(bf16[2,2,128,512]{2,3,1,0:T(8,128)(2,1)} %pad_maximum_fusion.2), channel_id=1, source_target_pairs={{0,2},{1,3},{2,4},{3,5},{4,6},{5,7},{6,8},{7,9},{8,10},{9,11},{10,... | collective-permute-start | bytes 1572872 | tf_op jit(solution)/shard_map/ppermute | solution.py:20
  83.4 3.2 %copy-start.17 = (f32[4,8,128]{2,1,0:T(8,128)S(1)}, f32[4,8,128]{2,1,0:T(8,128)}, u32[]{:S(2)}) copy-start(f32[4,8,128]{2,1,0:T(8,128)} %copy-done.16) | copy-start | bytes 49156
  93.6 6.1 %copy-start.5 = (bf16[1,1,128,512]{2,3,1,0:T(8,128)(2,1)S(1)}, bf16[1,1,128,512]{2,3,1,0:T(8,128)(2,1)}, u32[]{:S(2)}) copy-start(bf16[1,1,128,512]{2,3,1,0:T(8,128)(2,1)} %get-tuple-element.314) | copy-start | bytes 393220
  112.6 4.6 %copy-start.12 = (f32[128,4,8]{0,2,1:T(8,128)}, f32[128,4,8]{0,2,1:T(8,128)S(1)}, u32[]{:S(2)}) copy-start(f32[128,4,8]{0,2,1:T(8,128)S(1)} %get-tuple-element.284) | copy-start | bytes 49156
  115.2 42.7 %collective-permute-start.3 = (f32[1,2,128,512]{3,2,1,0:T(8,128)}, f32[1,2,128,512]{3,2,1,0:T(8,128)}, u32[]{:S(2)}, u32[]{:S(2)}) collective-permute-start(f32[1,2,128,512]{3,2,1,0:T(8,128)} %bitcast.607), channel_id=1, source_target_pairs={{4,0},{5,1},{6,2},{7,3},{8,4},{9,5},{10,6},{11,7},{12,8},{13,9},{1... | collective-permute-start | bytes 1572872 | tf_op jit(solution)/shard_map/ppermute | solution.py:20
  117.2 1.5 copy-start.13
  118.2 0.7 copy-start.6
  129.9 1.7 copy-start.14
  130.9 0.7 copy-start.7
  139.0 3.0 %copy-start.4 = (f32[1,2,128,512]{3,2,1,0:T(8,128)S(1)}, f32[1,2,128,512]{3,2,1,0:T(8,128)}, u32[]{:S(2)}) copy-start(f32[1,2,128,512]{3,2,1,0:T(8,128)} %copy.452) | copy-start | bytes 1572868 | tf_op jit(solution)/shard_map/cond
  141.9 4.4 %copy-start = (f32[4,8,128,128]{2,3,1,0:T(8,128)S(1)}, f32[4,8,128,128]{2,3,1,0:T(8,128)}, u32[]{:S(2)}) copy-start(f32[4,8,128,128]{2,3,1,0:T(8,128)} %get-tuple-element.322) | copy-start | bytes 6291460
  144.2 26.3 %collective-permute-start.4 = (f32[2,2,128,512]{3,2,1,0:T(8,128)}, f32[2,2,128,512]{3,2,1,0:T(8,128)}, u32[]{:S(2)}, u32[]{:S(2)}) collective-permute-start(f32[2,2,128,512]{3,2,1,0:T(8,128)} %pad_maximum_fusion.1), channel_id=1, source_target_pairs={{2,0},{3,1},{4,2},{5,3},{6,4},{7,5},{8,6},{9,7},{10,8},{11,9},{12,... | collective-permute-start | bytes 3145736 | tf_op jit(solution)/shard_map/ppermute | solution.py:20
  172.9 17.2 %collective-permute-start.5 = (f32[1,2,128,512]{3,2,1,0:T(8,128)}, f32[1,2,128,512]{3,2,1,0:T(8,128)}, u32[]{:S(2)}, u32[]{:S(2)}) collective-permute-start(f32[1,2,128,512]{3,2,1,0:T(8,128)} %slice.146), channel_id=1, source_target_pairs={{1,0},{2,1},{3,2},{4,3},{5,4},{6,5},{7,6},{8,7},{9,8},{10,9},{11,1... | collective-permute-start | bytes 1572872 | tf_op jit(solution)/shard_map/ppermute | solution.py:20
  179.8 1.3 copy-start.3
where the time goes:
time: 196 us; the launch traced here: 192 us
  local copies, waits for them, and re-layouts  45.6 us (23%)
  other arithmetic  34.3 us (17%)
  blocking collectives  33 us (17%)
  matrix products  29.1 us (15%)
  waiting for transfers between devices  27 us (14%)
  starting transfers between devices  14.9 us (8%)
  between operations  7.82 us (4%)
    psum x1, blocking collectives, per_device(): margins = lax.psum(member * own_margin, 'ctx')  29.9 us
    ppermute x6, waiting for transfers between devices, from_behind(): return lax.ppermute(shard, axis, pairs)  27 us
    ppermute x6, starting transfers between devices, from_behind(): return lax.ppermute(shard, axis, pairs)  14.9 us
    cond x5, local copies, waits for them, and re-layouts, per_device(): lax.cond(live_tiles[start_shift], partial(backward_block, start_shift), e...  11 us
    dot_general x3, matrix products, forward_block(): jnp.einsum('hgij,jhc->ihgc', rounded, value_block(start_shift), preferred...  7.7 us
    another operation x9, local copies, waits for them, and re-layouts  7.67 us
    reduce_sum x1, other arithmetic, per_device(): jnp.sum(group_heads.astype(jnp.float32) * output_sum, axis=-1)  6.37 us
    unnamed x31, local copies, waits for them, and re-layouts  6.05 us
  transfers between devices with their start and end apart: 6, of which 3 were waited for; matrix products, arithmetic and copies ran while one was open for 34% of the time, Pallas kernels for 0%

commit v1 on v0

v1 whole, which is shorter than its diff:
```python
import functools
import math

import jax
import jax.numpy as jnp
from jax import lax
from jax.experimental import pallas as pl
from jax.experimental.pallas import tpu as pltpu
from jax.sharding import PartitionSpec as P

QUERY_HEADS = 32
KEY_VALUE_HEADS = 4
HEAD_SIZE = 128
MAX_TILES = 5

preference_beta = 0.3

GROUP_HEADS = QUERY_HEADS // KEY_VALUE_HEADS
PAIR = 2
REACH = MAX_TILES - 1
SLOTS = MAX_TILES - 1
F32 = jnp.float32
BF16 = jnp.bfloat16
MESH = pl.DeviceIdType.MESH
NT = (((1,), (1,)), ((), ()))


def tile_facts(spans_ref, examples, position):
    start = jnp.int32(0)
    own_example = jnp.int32(0)
    own_start = jnp.int32(0)
    own_prompt = jnp.int32(0)
    own_chosen = jnp.int32(0)
    for e in range(examples):
        prompt, chosen, rejected = spans_ref[e, 0], spans_ref[e, 1], spans_ref[e, 2]
        here = position >= start
        own_example = jnp.where(here, e, own_example)
        own_start = jnp.where(here, start, own_start)
        own_prompt = jnp.where(here, prompt, own_prompt)
        own_chosen = jnp.where(here, chosen, own_chosen)
        start = start + prompt + chosen + rejected
    return own_example, own_start, own_prompt, own_chosen


def kernel(
    n_ctx, n_grp, examples, tile,
    spans_ref, terms_ref, q_hbm, k_hbm, v_hbm, du_hbm,
    att_hbm, dq_hbm, dk_ref, dv_ref,
    q_buf, du_buf, att_buf, dq_buf, kv_buf, gsend, grecv, own_grad, marg, rows,
    q_sem, du_sem, k_sem, v_sem, att_sem, dq_sem,
    kv_send, kv_recv, g_send, g_recv, m_send, m_recv, r_send, r_recv,
):
    me = lax.axis_index("ctx")
    grp = lax.axis_index("grp")
    width = GROUP_HEADS * HEAD_SIZE
    score_scale = HEAD_SIZE ** (-0.5)

    def own_copy(hbm, sem, which, g):
        return pltpu.make_async_copy(
            hbm.at[:, pl.ds(g * HEAD_SIZE, HEAD_SIZE)],
            kv_buf.at[g, which, pl.ds(0, tile)], sem.at[g])

    def wide_copy(hbm, buf, sem, g):
        return pltpu.make_async_copy(hbm.at[:, pl.ds(g * width, width)], buf.at[g], sem.at[g])

    for g in range(KEY_VALUE_HEADS):
        own_copy(k_hbm, k_sem, 0, g).start()
        own_copy(v_hbm, v_sem, 1, g).start()
    for g in range(KEY_VALUE_HEADS):
        wide_copy(q_hbm, q_buf, q_sem, g).start()
        wide_copy(du_hbm, du_buf, du_sem, g).start()

    barrier = pltpu.get_barrier_semaphore()

    def greet_ctx(o, carry):
        pl.semaphore_signal(
            barrier, inc=1, device_id=(grp, lax.rem(me + o, n_ctx)), device_id_type=MESH)
        return carry

    def greet_grp(o, carry):
        pl.semaphore_signal(
            barrier, inc=1, device_id=(lax.rem(grp + o, n_grp), me), device_id_type=MESH)
        return carry

    lax.fori_loop(1, n_ctx, greet_ctx, 0)
    lax.fori_loop(1, n_grp, greet_grp, 0)

    own_example, own_start, own_prompt, own_chosen = tile_facts(spans_ref, examples, me)
    within = me - own_start
    is_rejected = within >= own_prompt + own_chosen
    is_chosen = jnp.logical_and(within >= own_prompt, jnp.logical_not(is_rejected))
    polarity = jnp.where(is_chosen, 1.0, jnp.where(is_rejected, -1.0, 0.0)).astype(F32)
    live = []
    for d in range(1, MAX_TILES):
        w = within - d
        blocked = jnp.logical_and(
            is_rejected, jnp.logical_and(w >= own_prompt, w < own_prompt + own_chosen))
        live.append(jnp.where(jnp.logical_and(w >= 0, jnp.logical_not(blocked)), 1.0, 0.0).astype(F32))
    spare = live[REACH - 1]
    swap = []
    for d in range(1, SLOTS):
        taken = spare * (1.0 - live[d - 1])
        swap.append(taken)
        spare = spare - taken
    bias = [jnp.where(live[d - 1] + swap[d - 1] > 0.5, 0.0, -jnp.inf).astype(F32)
            for d in range(1, SLOTS)]

    lanes = lax.broadcasted_iota(jnp.int32, (8, 128), 1)
    mine = lanes == own_example
    own_sum = jnp.sum(terms_ref[...], axis=-1, keepdims=True) * polarity
    marg[n_ctx - 1] = jnp.where(mine, jnp.broadcast_to(own_sum, (8, 128)), 0.0)

    for d in range(1, MAX_TILES):
        @pl.when(me < d)
        def _():
            kv_buf[:, :, d * tile:(d + 1) * tile, :] = jnp.zeros(
                (KEY_VALUE_HEADS, 2, tile, HEAD_SIZE), BF16)

        @pl.when(me + d >= n_ctx)
        def _():
            grecv[:, d - 1] = jnp.zeros((KEY_VALUE_HEADS, 2, tile, HEAD_SIZE), BF16)

    pl.semaphore_wait(barrier, n_ctx - 1 + n_grp - 1)

    def margin_copy(o):
        return pltpu.make_async_remote_copy(
            src_ref=marg.at[n_ctx - 1], dst_ref=marg.at[o - 1],
            send_sem=m_send.at[o - 1], recv_sem=m_recv.at[o - 1],
            device_id=(grp, lax.rem(me + o, n_ctx)), device_id_type=MESH)

    def row_copy(o):
        return pltpu.make_async_remote_copy(
            src_ref=rows.at[n_grp - 1], dst_ref=rows.at[o - 1],
            send_sem=r_send.at[o - 1], recv_sem=r_recv.at[o - 1],
            device_id=(lax.rem(grp + o, n_grp), me), device_id_type=MESH)

    def kv_copy(g, d):
        return pltpu.make_async_remote_copy(
            src_ref=kv_buf.at[g, :, pl.ds(0, tile)],
            dst_ref=kv_buf.at[g, :, pl.ds(d * tile, tile)],
            send_sem=kv_send.at[g, d - 1], recv_sem=kv_recv.at[g, d - 1],
            device_id=(grp, jnp.minimum(me + d, n_ctx - 1)), device_id_type=MESH)

    def grad_copy(g, d):
        return pltpu.make_async_remote_copy(
            src_ref=gsend.at[g, d - 1],
            dst_ref=grecv.at[g, d - 1],
            send_sem=g_send.at[g, d - 1], recv_sem=g_recv.at[g, d - 1],
            device_id=(grp, jnp.maximum(me - d, 0)), device_id_type=MESH)

    def loop(low, high, act):
        def body(o, carry):
            act(o)
            return carry
        lax.fori_loop(low, high, body, 0)

    loop(1, n_ctx, lambda o: margin_copy(o).start())
    for g in range(KEY_VALUE_HEADS):
        own_copy(k_hbm, k_sem, 0, g).wait()
        own_copy(v_hbm, v_sem, 1, g).wait()
        for d in range(1, MAX_TILES):
            @pl.when(me + d < n_ctx)
            def _():
                kv_copy(g, d).start()

    loop(1, n_ctx, lambda o: margin_copy(o).wait_recv())
    margins = jnp.sum(marg[...], axis=0)
    rows[n_grp - 1] = jnp.broadcast_to(jnp.sum(margins, axis=-1, keepdims=True), (8, 128))
    loop(1, n_grp, lambda o: row_copy(o).start())
    loop(1, n_grp, lambda o: row_copy(o).wait_recv())
    center = jnp.sum(rows[...], axis=0) / (examples * n_grp)
    weights = jax.nn.sigmoid(preference_beta * (center - margins))
    own_weight = jnp.sum(jnp.where(mine, weights, 0.0), axis=-1, keepdims=True)[:1]

    causal = (lax.broadcasted_iota(jnp.int32, (tile, PAIR * tile), 0)
              <= lax.rem(lax.broadcasted_iota(jnp.int32, (tile, PAIR * tile), 1), tile))

    def group(g, carry):
        wide_copy(q_hbm, q_buf, q_sem, g).wait()
        wide_copy(du_hbm, du_buf, du_sem, g).wait()
        for d in range(1, MAX_TILES):
            @pl.when(me >= d)
            def _():
                kv_copy(g, d).wait_recv()

        def merged(which):
            far = kv_buf[g, which, REACH * tile:(REACH + 1) * tile].astype(F32)
            parts = [kv_buf[g, which, 0:tile]]
            for d in range(1, SLOTS):
                near = kv_buf[g, which, d * tile:(d + 1) * tile].astype(F32)
                parts.append((near * (1.0 - swap[d - 1]) + far * swap[d - 1]).astype(BF16))
            return jnp.concatenate(parts, axis=0)

        keys = merged(0)
        values = merged(1)
        keys_t = keys.T
        values_t = values.T
        q_all, cot_all, prob_all, ds_all = [], [], [], []
        for p in range(GROUP_HEADS // PAIR):
            cols = [slice((p * PAIR + h) * HEAD_SIZE, (p * PAIR + h + 1) * HEAD_SIZE)
                    for h in range(PAIR)]
            q = jnp.concatenate([q_buf[g, :, c] for c in cols], axis=0)
            cot = (jnp.concatenate([du_buf[g, :, c] for c in cols], axis=0).astype(F32)
                   * own_weight).astype(BF16)
            raw = lax.dot_general(keys, q, NT, preferred_element_type=F32)
            raw = raw * (score_scale * math.log2(math.e))
            pieces = [jnp.where(causal, raw[:tile], -jnp.inf)]
            for d in range(1, SLOTS):
                pieces.append(raw[d * tile:(d + 1) * tile] + bias[d - 1])
            scores = jnp.concatenate(pieces, axis=0)
            top = jnp.max(scores, axis=0, keepdims=True)
            powers = jnp.exp2(scores - top)
            inverse = 1.0 / jnp.sum(powers, axis=0, keepdims=True)
            prob = powers * inverse
            rounded = prob.astype(BF16)
            out_t = jnp.dot(values_t, rounded, preferred_element_type=F32)
            dprob = lax.dot_general(values, cot, NT, preferred_element_type=F32)
            dots = jnp.sum(rounded.astype(F32) * dprob, axis=0, keepdims=True)
            ds = (prob * (dprob - dots) * score_scale).astype(BF16)
            dq_t = jnp.dot(keys_t, ds, preferred_element_type=F32)
            for h in range(PAIR):
                att_buf[g, :, cols[h]] = out_t[:, h * tile:(h + 1) * tile].T.astype(BF16)
                dq_buf[g, :, cols[h]] = dq_t[:, h * tile:(h + 1) * tile].T.astype(BF16)
            q_all.append(q)
            cot_all.append(cot)
            prob_all.append(rounded)
            ds_all.append(ds)
        dk = jnp.dot(jnp.concatenate(ds_all, axis=1), jnp.concatenate(q_all, axis=0),
                     preferred_element_type=F32)
        dv = jnp.dot(jnp.concatenate(prob_all, axis=1), jnp.concatenate(cot_all, axis=0),
                     preferred_element_type=F32)
        pltpu.make_async_copy(att_buf.at[g], att_hbm.at[:, pl.ds(g * width, width)], att_sem.at[g]).start()
        pltpu.make_async_copy(dq_buf.at[g], dq_hbm.at[:, pl.ds(g * width, width)], dq_sem.at[g]).start()
        for which, grad in ((0, dk), (1, dv)):
            own_grad[g, which] = grad[:tile]
            far = jnp.zeros((tile, HEAD_SIZE), F32)
            for d in range(1, SLOTS):
                part = grad[d * tile:(d + 1) * tile]
                gsend[g, d - 1, which] = (part * (1.0 - swap[d - 1])).astype(BF16)
                far = far + part * swap[d - 1]
            gsend[g, REACH - 1, which] = far.astype(BF16)
        for d in range(1, MAX_TILES):
            @pl.when(me >= d)
            def _():
                grad_copy(g, d).start()
        return carry

    lax.fori_loop(0, KEY_VALUE_HEADS, group, 0)

    for g in range(KEY_VALUE_HEADS):
        for d in range(1, MAX_TILES):
            @pl.when(me + d < n_ctx)
            def _():
                kv_copy(g, d).wait_send()
                grad_copy(g, d).wait_recv()
        for which, out in ((0, dk_ref), (1, dv_ref)):
            total = own_grad[g, which]
            for d in range(1, MAX_TILES):
                total = total + grecv[g, d - 1, which].astype(F32)
            out[:, g * HEAD_SIZE:(g + 1) * HEAD_SIZE] = total.astype(BF16)
    for g in range(KEY_VALUE_HEADS):
        pltpu.make_async_copy(att_buf.at[g], att_hbm.at[:, pl.ds(g * width, width)], att_sem.at[g]).wait()
        pltpu.make_async_copy(dq_buf.at[g], dq_hbm.at[:, pl.ds(g * width, width)], dq_sem.at[g]).wait()
        for d in range(1, MAX_TILES):
            @pl.when(me >= d)
            def _():
                grad_copy(g, d).wait_send()
    loop(1, n_ctx, lambda o: margin_copy(o).wait_send())
    loop(1, n_grp, lambda o: row_copy(o).wait_send())


def per_device(queries, keys, values, d_unit, token_terms, spans):
    tile = queries.shape[0]
    n_ctx = lax.axis_size("ctx")
    n_grp = lax.axis_size("grp")
    width = GROUP_HEADS * HEAD_SIZE
    wide = pltpu.VMEM((KEY_VALUE_HEADS, tile, width), BF16)
    slots = pltpu.VMEM((KEY_VALUE_HEADS, REACH, 2, tile, HEAD_SIZE), BF16)
    dma = pltpu.SemaphoreType.DMA
    groups = dma((KEY_VALUE_HEADS,))
    per_slot = dma((KEY_VALUE_HEADS, REACH))
    anywhere = pl.BlockSpec(memory_space=pl.ANY)
    vmem = pl.BlockSpec(memory_space=pltpu.VMEM)
    flops = 12 * QUERY_HEADS * tile * tile * HEAD_SIZE * SLOTS
    return pl.pallas_call(
        functools.partial(kernel, n_ctx, n_grp, spans.shape[0], tile),
        out_shape=(
            jax.ShapeDtypeStruct(queries.shape, BF16),
            jax.ShapeDtypeStruct(queries.shape, BF16),
            jax.ShapeDtypeStruct(keys.shape, BF16),
            jax.ShapeDtypeStruct(values.shape, BF16),
        ),
        in_specs=[pl.BlockSpec(memory_space=pltpu.SMEM), vmem] + [anywhere] * 4,
        out_specs=(anywhere, anywhere, vmem, vmem),
        scratch_shapes=[
            wide, wide, wide, wide,
            pltpu.VMEM((KEY_VALUE_HEADS, 2, MAX_TILES * tile, HEAD_SIZE), BF16),
            slots, slots,
            pltpu.VMEM((KEY_VALUE_HEADS, 2, tile, HEAD_SIZE), F32),
            pltpu.VMEM((n_ctx, 8, 128), F32),
            pltpu.VMEM((n_grp, 8, 128), F32),
            groups, groups, groups, groups, groups, groups,
            per_slot, per_slot, per_slot, per_slot,
            dma((max(n_ctx - 1, 1),)), dma((max(n_ctx - 1, 1),)),
            dma((max(n_grp - 1, 1),)), dma((max(n_grp - 1, 1),)),
        ],
        compiler_params=pltpu.CompilerParams(
            collective_id=0, has_side_effects=True, vmem_limit_bytes=48 * 1024 * 1024),
        cost_estimate=pl.CostEstimate(
            flops=flops, bytes_accessed=8 * queries.size,
            transcendentals=QUERY_HEADS * tile * tile * SLOTS),
    )(spans, token_terms.reshape(1, tile), queries, keys, values, d_unit)


def solution(mesh):
    return jax.shard_map(
        per_device,
        mesh=mesh,
        in_specs=(
            P(("grp", "ctx"), None),
            P(("grp", "ctx"), None),
            P(("grp", "ctx"), None),
            P(("grp", "ctx"), None),
            P(("grp", "ctx")),
            P("grp", None),
        ),
        out_specs=(
            P(("grp", "ctx"), None),
            P(("grp", "ctx"), None),
            P(("grp", "ctx"), None),
            P(("grp", "ctx"), None),
        ),
        check_vma=False,
    )
```

time: 196 us -> 52.3 us (0.27)
  the two profiles are of different devices: /device:TPU:18 before, /device:TPU:0 now
where the time goes in v1:
time: 52.3 us; the launch traced here: 52.1 us
  Pallas kernels  42.6 us (81%)
  local copies, waits for them, and re-layouts  8.84 us (17%)
  between operations  0.66 us (1%)
    pallas_call x1, Pallas kernels, per_device(): pl.pallas_call(functools.partial(kernel, n_ctx, n_grp, spans.shape[0], ti...  42.6 us
    unnamed x16, local copies, waits for them, and re-layouts  8.84 us

profile of v1, /device:TPU:0, one launch (start us, length us, event | category | flops | bytes accessed | tf_op | source)
XLA Modules:
  0.0 52.1 jit_solution(16930078572896490521)
XLA Ops:
  0.6 0.0 copy-start.5
  0.6 0.6 %copy-done.5 = f32[128]{0:T(128)S(1)} copy-done((f32[128]{0:T(128)S(1)}, f32[128]{0:T(128)}, u32[]{:S(2)}) %copy-start.5) | copy-done | bytes 536
  1.3 0.0 copy-start
  1.3 1.2 %copy-done = bf16[128,4096]{1,0:T(8,128)(2,1)S(1)} copy-done((bf16[128,4096]{1,0:T(8,128)(2,1)S(1)}, bf16[128,4096]{1,0:T(8,128)(2,1)}, u32[]{:S(2)}) %copy-start) | copy-done | bytes 1048600
  2.5 0.0 copy-start.1
  2.5 1.2 %copy-done.1 = bf16[128,4096]{1,0:T(8,128)(2,1)S(1)} copy-done((bf16[128,4096]{1,0:T(8,128)(2,1)S(1)}, bf16[128,4096]{1,0:T(8,128)(2,1)}, u32[]{:S(2)}) %copy-start.1) | copy-done | bytes 1048600
  3.7 0.0 copy-start.2
  3.7 0.9 %copy-done.2 = bf16[128,512]{1,0:T(8,128)(2,1)S(1)} copy-done((bf16[128,512]{1,0:T(8,128)(2,1)S(1)}, bf16[128,512]{1,0:T(8,128)(2,1)}, u32[]{:S(2)}) %copy-start.2) | copy-done | bytes 131096
  4.6 0.0 copy-start.3
  4.6 0.9 %copy-done.3 = bf16[128,512]{1,0:T(8,128)(2,1)S(1)} copy-done((bf16[128,512]{1,0:T(8,128)(2,1)S(1)}, bf16[128,512]{1,0:T(8,128)(2,1)}, u32[]{:S(2)}) %copy-start.3) | copy-done | bytes 131096
  5.5 0.0 copy-start.4
  5.6 0.7 %copy-done.4 = s32[4,3]{1,0:T(4,128)S(1)} copy-done((s32[4,3]{1,0:T(4,128)S(1)}, s32[4,3]{1,0:T(4,128)}, u32[]{:S(2)}) %copy-start.4) | copy-done | bytes 72
  6.2 42.6 %shard_map.93 = (bf16[128,4096]{1,0:T(8,128)(2,1)S(1)}, bf16[128,4096]{1,0:T(8,128)(2,1)S(1)}, bf16[128,512]{1,0:T(8,128)(2,1)S(1)}, bf16[128,512]{1,0:T(8,128)(2,1)S(1)}) custom-call(s32[4,3]{1,0:T(4,128)S(1)} %copy-done.4, f32[1,128]{1,0:T(1,128)S(1)} %bitcast.1, bf16[128,4096]{1,0:T(8,128)(2,1)S(1)} %copy-done, bf16[128,512]{1,0:T(8,128)(2,1)S(1)} %copy-done.2, ...), custom_call_target="tpu_custom_call" | custom-call | flops 3221225472 | bytes 4194304 | tf_op jit(solution)/shard_map/pallas_call | solution.py:285
  48.8 1.0 %copy.14 = bf16[128,4096]{1,0:T(8,128)(2,1)} copy(bf16[128,4096]{1,0:T(8,128)(2,1)S(1)} %get-tuple-element.8) | data formatting | bytes 2097152
  49.8 1.0 %copy.15 = bf16[128,4096]{1,0:T(8,128)(2,1)} copy(bf16[128,4096]{1,0:T(8,128)(2,1)S(1)} %get-tuple-element.9) | data formatting | bytes 2097152
  50.7 0.7 %copy.16 = bf16[128,512]{1,0:T(8,128)(2,1)} copy(bf16[128,512]{1,0:T(8,128)(2,1)S(1)} %get-tuple-element.10) | data formatting | bytes 262144
  51.4 0.7 %copy.17 = bf16[128,512]{1,0:T(8,128)(2,1)} copy(bf16[128,512]{1,0:T(8,128)(2,1)S(1)} %get-tuple-element.11) | data formatting | bytes 262144
Async XLA Ops:
  0.6 0.7 %copy-start.5 = (f32[128]{0:T(128)S(1)}, f32[128]{0:T(128)}, u32[]{:S(2)}) copy-start(f32[128]{0:T(128)} %param.10) | copy-start | bytes 1540
  1.3 1.2 %copy-start = (bf16[128,4096]{1,0:T(8,128)(2,1)S(1)}, bf16[128,4096]{1,0:T(8,128)(2,1)}, u32[]{:S(2)}) copy-start(bf16[128,4096]{1,0:T(8,128)(2,1)} %q_hbm.1) | copy-start | bytes 3145732
  2.5 1.2 %copy-start.1 = (bf16[128,4096]{1,0:T(8,128)(2,1)S(1)}, bf16[128,4096]{1,0:T(8,128)(2,1)}, u32[]{:S(2)}) copy-start(bf16[128,4096]{1,0:T(8,128)(2,1)} %du_hbm.1) | copy-start | bytes 3145732
  3.7 0.9 %copy-start.2 = (bf16[128,512]{1,0:T(8,128)(2,1)S(1)}, bf16[128,512]{1,0:T(8,128)(2,1)}, u32[]{:S(2)}) copy-start(bf16[128,512]{1,0:T(8,128)(2,1)} %k_hbm.1) | copy-start | bytes 393220
  4.6 0.9 %copy-start.3 = (bf16[128,512]{1,0:T(8,128)(2,1)S(1)}, bf16[128,512]{1,0:T(8,128)(2,1)}, u32[]{:S(2)}) copy-start(bf16[128,512]{1,0:T(8,128)(2,1)} %v_hbm.1) | copy-start | bytes 393220
  5.5 0.7 %copy-start.4 = (s32[4,3]{1,0:T(4,128)S(1)}, s32[4,3]{1,0:T(4,128)}, u32[]{:S(2)}) copy-start(s32[4,3]{1,0:T(4,128)} %spans_ref.1) | copy-start | bytes 148

commit v2 on v1

--- a/solution.py
+++ b/solution.py
@@ -44,10 +44,10 @@
 
 def kernel(
     n_ctx, n_grp, examples, tile,
-    spans_ref, terms_ref, q_hbm, k_hbm, v_hbm, du_hbm,
-    att_hbm, dq_hbm, dk_ref, dv_ref,
-    q_buf, du_buf, att_buf, dq_buf, kv_buf, gsend, grecv, own_grad, marg, rows,
-    q_sem, du_sem, k_sem, v_sem, att_sem, dq_sem,
+    spans_hbm, terms_hbm, q_hbm, k_hbm, v_hbm, du_hbm,
+    att_hbm, dq_hbm, dk_hbm, dv_hbm,
+    spans_ref, terms_ref, dk_ref, dv_ref, q_buf, du_buf, att_buf, dq_buf, kv_buf, gsend, grecv, own_grad, marg, rows,
+    small_sem, q_sem, du_sem, k_sem, v_sem, att_sem, dq_sem,
     kv_send, kv_recv, g_send, g_recv, m_send, m_recv, r_send, r_recv,
 ):
     me = lax.axis_index("ctx")
@@ -63,6 +63,10 @@
     def wide_copy(hbm, buf, sem, g):
         return pltpu.make_async_copy(hbm.at[:, pl.ds(g * width, width)], buf.at[g], sem.at[g])
 
+    spans_copy = pltpu.make_async_copy(spans_hbm, spans_ref, small_sem.at[0])
+    terms_copy = pltpu.make_async_copy(terms_hbm, terms_ref, small_sem.at[1])
+    spans_copy.start()
+    terms_copy.start()
     for g in range(KEY_VALUE_HEADS):
         own_copy(k_hbm, k_sem, 0, g).start()
         own_copy(v_hbm, v_sem, 1, g).start()
@@ -85,6 +89,8 @@
     lax.fori_loop(1, n_ctx, greet_ctx, 0)
     lax.fori_loop(1, n_grp, greet_grp, 0)
 
+    spans_copy.wait()
+    terms_copy.wait()
     own_example, own_start, own_prompt, own_chosen = tile_facts(spans_ref, examples, me)
     within = me - own_start
     is_rejected = within >= own_prompt + own_chosen
@@ -195,40 +201,69 @@
         values = merged(1)
         keys_t = keys.T
         values_t = values.T
-        q_all, cot_all, prob_all, ds_all = [], [], [], []
-        for p in range(GROUP_HEADS // PAIR):
-            cols = [slice((p * PAIR + h) * HEAD_SIZE, (p * PAIR + h + 1) * HEAD_SIZE)
+        pairs = GROUP_HEADS // PAIR
+
+        def columns(p):
+            return [slice((p * PAIR + h) * HEAD_SIZE, (p * PAIR + h + 1) * HEAD_SIZE)
                     for h in range(PAIR)]
-            q = jnp.concatenate([q_buf[g, :, c] for c in cols], axis=0)
-            cot = (jnp.concatenate([du_buf[g, :, c] for c in cols], axis=0).astype(F32)
+
+        def products(p):
+            q = jnp.concatenate([q_buf[g, :, c] for c in columns(p)], axis=0)
+            cot = (jnp.concatenate([du_buf[g, :, c] for c in columns(p)], axis=0).astype(F32)
                    * own_weight).astype(BF16)
-            raw = lax.dot_general(keys, q, NT, preferred_element_type=F32)
-            raw = raw * (score_scale * math.log2(math.e))
-            pieces = [jnp.where(causal, raw[:tile], -jnp.inf)]
+            return (q, cot, lax.dot_general(keys, q, NT, preferred_element_type=F32),
+                    lax.dot_general(values, cot, NT, preferred_element_type=F32))
+
+        def slot(x, d):
+            return x[d * tile:(d + 1) * tile]
+
+        def softmax(raw, dprob):
+            near = jnp.where(causal, slot(raw, 0), -jnp.inf)
+            blocks = [near] + [slot(raw, d) for d in range(1, SLOTS)]
+            tops = [jnp.max(block, axis=0, keepdims=True) for block in blocks]
+            top = tops[0]
             for d in range(1, SLOTS):
-                pieces.append(raw[d * tile:(d + 1) * tile] + bias[d - 1])
-            scores = jnp.concatenate(pieces, axis=0)
-            top = jnp.max(scores, axis=0, keepdims=True)
-            powers = jnp.exp2(scores - top)
-            inverse = 1.0 / jnp.sum(powers, axis=0, keepdims=True)
-            prob = powers * inverse
-            rounded = prob.astype(BF16)
-            out_t = jnp.dot(values_t, rounded, preferred_element_type=F32)
-            dprob = lax.dot_general(values, cot, NT, preferred_element_type=F32)
-            dots = jnp.sum(rounded.astype(F32) * dprob, axis=0, keepdims=True)
-            ds = (prob * (dprob - dots) * score_scale).astype(BF16)
-            dq_t = jnp.dot(keys_t, ds, preferred_element_type=F32)
-            for h in range(PAIR):
-                att_buf[g, :, cols[h]] = out_t[:, h * tile:(h + 1) * tile].T.astype(BF16)
-                dq_buf[g, :, cols[h]] = dq_t[:, h * tile:(h + 1) * tile].T.astype(BF16)
-            q_all.append(q)
-            cot_all.append(cot)
-            prob_all.append(rounded)
-            ds_all.append(ds)
-        dk = jnp.dot(jnp.concatenate(ds_all, axis=1), jnp.concatenate(q_all, axis=0),
-                     preferred_element_type=F32)
-        dv = jnp.dot(jnp.concatenate(prob_all, axis=1), jnp.concatenate(cot_all, axis=0),
-                     preferred_element_type=F32)
+                top = jnp.maximum(top, tops[d] + bias[d - 1])
+            powers, total, dots = [], 0.0, 0.0
+            for d in range(SLOTS):
+                level = top if d == 0 else top - bias[d - 1]
+                power = jnp.exp2((blocks[d] - level) * (score_scale * math.log2(math.e)))
+                total = total + jnp.sum(power, axis=0, keepdims=True)
+                dots = dots + jnp.sum(power * slot(dprob, d), axis=0, keepdims=True)
+                powers.append(power)
+            inverse = 1.0 / total
+            dots = dots * inverse
+            rounded, ds = [], []
+            for d in range(SLOTS):
+                prob = powers[d] * inverse
+                rounded.append(prob.astype(BF16))
+                ds.append((prob * (slot(dprob, d) - dots)).astype(BF16))
+            return jnp.concatenate(rounded, axis=0), jnp.concatenate(ds, axis=0)
+
+        ahead = products(0)
+        dk = dv = None
+        kept = []
+        for p in range(pairs):
+            q, cot, raw, dprob = ahead
+            if p + 1 < pairs:
+                ahead = products(p + 1)
+            rounded, ds = softmax(raw, dprob)
+            kept.append((q, cot, rounded, ds))
+            out_t = jnp.dot(values_t, rounded, preferred_element_type=F32).astype(BF16)
+            dq_t = (jnp.dot(keys_t, ds, preferred_element_type=F32) * score_scale).astype(BF16)
+            for h, c in enumerate(columns(p)):
+                att_buf[g, :, c] = out_t[:, h * tile:(h + 1) * tile].T
+                dq_buf[g, :, c] = dq_t[:, h * tile:(h + 1) * tile].T
+            if p % 2 == 1:
+                qs, cots, probs, dss = zip(*kept)
+                kept = []
+                dk_part = jnp.dot(jnp.concatenate(dss, axis=1), jnp.concatenate(qs, axis=0),
+                                  preferred_element_type=F32)
+                dv_part = jnp.dot(jnp.concatenate(probs, axis=1), jnp.concatenate(cots, axis=0),
+                                  preferred_element_type=F32)
+                dk = dk_part if dk is None else dk + dk_part
+                dv = dv_part if dv is None else dv + dv_part
+        dk = dk * score_scale
         pltpu.make_async_copy(att_buf.at[g], att_hbm.at[:, pl.ds(g * width, width)], att_sem.at[g]).start()
         pltpu.make_async_copy(dq_buf.at[g], dq_hbm.at[:, pl.ds(g * width, width)], dq_sem.at[g]).start()
         for which, grad in ((0, dk), (1, dv)):
@@ -258,6 +293,10 @@
             for d in range(1, MAX_TILES):
                 total = total + grecv[g, d - 1, which].astype(F32)
             out[:, g * HEAD_SIZE:(g + 1) * HEAD_SIZE] = total.astype(BF16)
+    dk_copy = pltpu.make_async_copy(dk_ref, dk_hbm, small_sem.at[0])
+    dv_copy = pltpu.make_async_copy(dv_ref, dv_hbm, small_sem.at[1])
+    dk_copy.start()
+    dv_copy.start()
     for g in range(KEY_VALUE_HEADS):
         pltpu.make_async_copy(att_buf.at[g], att_hbm.at[:, pl.ds(g * width, width)], att_sem.at[g]).wait()
         pltpu.make_async_copy(dq_buf.at[g], dq_hbm.at[:, pl.ds(g * width, width)], dq_sem.at[g]).wait()
@@ -265,8 +304,28 @@
             @pl.when(me >= d)
             def _():
                 grad_copy(g, d).wait_send()
+    dk_copy.wait()
+    dv_copy.wait()
     loop(1, n_ctx, lambda o: margin_copy(o).wait_send())
     loop(1, n_grp, lambda o: row_copy(o).wait_send())
+
+
+CUTS = 4
+VMEM_BYTES = 64 * 1024 * 1024
+
+
+def hand_over(*refs):
+    sources, targets, sem = refs[:4], refs[4:8], refs[8]
+    copies = []
+    for a, (source, target) in enumerate(zip(sources, targets)):
+        rows = source.shape[0] // CUTS
+        for c in range(CUTS):
+            part = pl.ds(c * rows, rows)
+            copies.append(pltpu.make_async_copy(source.at[part], target.at[part], sem.at[a, c]))
+    for copy in copies:
+        copy.start()
+    for copy in copies:
+        copy.wait()
 
 
 def per_device(queries, keys, values, d_unit, token_terms, spans):
@@ -279,10 +338,9 @@
     dma = pltpu.SemaphoreType.DMA
     groups = dma((KEY_VALUE_HEADS,))
     per_slot = dma((KEY_VALUE_HEADS, REACH))
-    anywhere = pl.BlockSpec(memory_space=pl.ANY)
-    vmem = pl.BlockSpec(memory_space=pltpu.VMEM)
+    hbm = pl.BlockSpec(memory_space=pltpu.HBM)
     flops = 12 * QUERY_HEADS * tile * tile * HEAD_SIZE * SLOTS
-    return pl.pallas_call(
+    found = pl.pallas_call(
         functools.partial(kernel, n_ctx, n_grp, spans.shape[0], tile),
         out_shape=(
             jax.ShapeDtypeStruct(queries.shape, BF16),
@@ -290,26 +348,39 @@
             jax.ShapeDtypeStruct(keys.shape, BF16),
             jax.ShapeDtypeStruct(values.shape, BF16),
         ),
-        in_specs=[pl.BlockSpec(memory_space=pltpu.SMEM), vmem] + [anywhere] * 4,
-        out_specs=(anywhere, anywhere, vmem, vmem),
+        in_specs=[hbm] * 6,
+        out_specs=(hbm, hbm, hbm, hbm),
         scratch_shapes=[
+            pltpu.SMEM(spans.shape, jnp.int32),
+            pltpu.VMEM((1, tile), F32),
+            pltpu.VMEM(keys.shape, BF16),
+            pltpu.VMEM(values.shape, BF16),
             wide, wide, wide, wide,
             pltpu.VMEM((KEY_VALUE_HEADS, 2, MAX_TILES * tile, HEAD_SIZE), BF16),
             slots, slots,
             pltpu.VMEM((KEY_VALUE_HEADS, 2, tile, HEAD_SIZE), F32),
             pltpu.VMEM((n_ctx, 8, 128), F32),
             pltpu.VMEM((n_grp, 8, 128), F32),
-            groups, groups, groups, groups, groups, groups,
+            dma((2,)), groups, groups, groups, groups, groups, groups,
             per_slot, per_slot, per_slot, per_slot,
             dma((max(n_ctx - 1, 1),)), dma((max(n_ctx - 1, 1),)),
             dma((max(n_grp - 1, 1),)), dma((max(n_grp - 1, 1),)),
         ],
         compiler_params=pltpu.CompilerParams(
-            collective_id=0, has_side_effects=True, vmem_limit_bytes=48 * 1024 * 1024),
+            collective_id=0, has_side_effects=True, vmem_limit_bytes=VMEM_BYTES),
         cost_estimate=pl.CostEstimate(
             flops=flops, bytes_accessed=8 * queries.size,
             transcendentals=QUERY_HEADS * tile * tile * SLOTS),
     )(spans, token_terms.reshape(1, tile), queries, keys, values, d_unit)
+    return pl.pallas_call(
+        hand_over,
+        out_shape=tuple(jax.ShapeDtypeStruct(x.shape, x.dtype) for x in found),
+        in_specs=[hbm] * 4,
+        out_specs=(hbm,) * 4,
+        scratch_shapes=[dma((4, CUTS))],
+        compiler_params=pltpu.CompilerParams(vmem_limit_bytes=VMEM_BYTES),
+        cost_estimate=pl.CostEstimate(flops=0, bytes_accessed=10 * queries.size, transcendentals=0),
+    )(*found)
 
 
 def solution(mesh):

time: 52.3 us -> 114 us (2.18)
  Pallas kernels: 42.6 us -> 113 us
  local copies, waits for them, and re-layouts: 8.84 us -> 0 us
    pallas_call x0 -> x1, Pallas kernels: none -> 72.7 us  [per_device(): pl.pallas_call(hand_over, out_shape=tuple((jax.ShapeDtypeStruct(x.shape,...]
    unnamed x16 -> x0, local copies, waits for them, and re-layouts: 8.84 us -> none
    pallas_call x1, Pallas kernels: 42.6 us -> 40.5 us  [per_device(): pl.pallas_call(functools.partial(kernel, n_ctx, n_grp, spans.shape[0], ti...]
where the time goes in v2:
time: 114 us
  Pallas kernels  113 us (99%)
    pallas_call x1, Pallas kernels, per_device(): pl.pallas_call(hand_over, out_shape=tuple((jax.ShapeDtypeStruct(x.shape,...  72.7 us
    pallas_call x1, Pallas kernels, per_device(): pl.pallas_call(functools.partial(kernel, n_ctx, n_grp, spans.shape[0], ti...  40.5 us

profile of v2, /device:TPU:0, one launch (start us, length us, event | category | flops | bytes accessed | tf_op | source)
XLA Modules:
  0.0 113.8 jit_solution(11931346210762075618)
XLA Ops:
  0.6 40.5 %shard_map.93 = (bf16[128,4096]{1,0:T(8,128)(2,1)}, bf16[128,4096]{1,0:T(8,128)(2,1)}, bf16[128,512]{1,0:T(8,128)(2,1)}, bf16[128,512]{1,0:T(8,128)(2,1)}) custom-call(s32[4,3]{1,0:T(4,128)} %spans_hbm.1, f32[1,128]{1,0:T(1,128)} %bitcast.1, bf16[128,4096]{1,0:T(8,128)(2,1)} %q_hbm.1, bf16[128,512]{1,0:T(8,128)(2,1)} %k_hbm.1, bf16[128,512]{1,0:T(8,128)(2,1)} %v_hbm.1, ...), custom_call_target="tpu_custom_call" | custom-call | flops 3221225472 | bytes 4194304 | tf_op jit(solution)/shard_map/pallas_call | solution.py:343
  41.1 72.7 %shard_map.94 = (bf16[128,4096]{1,0:T(8,128)(2,1)}, bf16[128,4096]{1,0:T(8,128)(2,1)}, bf16[128,512]{1,0:T(8,128)(2,1)}, bf16[128,512]{1,0:T(8,128)(2,1)}) custom-call(bf16[128,4096]{1,0:T(8,128)(2,1)} %get-tuple-element.8.refs_0_, bf16[128,4096]{1,0:T(8,128)(2,1)} %get-tuple-element.9.refs_1_, bf16[128,512]{1,0:T(8,128)(2,1)} %get-tuple-element.10.refs_2_, ...), custom_call_target="tpu_custom_call" | custom-call | bytes 5242880 | tf_op jit(solution)/shard_map/pallas_call | solution.py:375

commit v3 on v2

--- a/solution.py
+++ b/solution.py
@@ -315,16 +315,20 @@
 
 
 def hand_over(*refs):
-    sources, targets, sem = refs[:4], refs[4:8], refs[8]
-    copies = []
-    for a, (source, target) in enumerate(zip(sources, targets)):
+    sources, targets, stages, in_sem, out_sem = refs[:4], refs[4:8], refs[8:12], refs[12], refs[13]
+    arriving, leaving = [], []
+    for a, (source, target, stage) in enumerate(zip(sources, targets, stages)):
         rows = source.shape[0] // CUTS
         for c in range(CUTS):
             part = pl.ds(c * rows, rows)
-            copies.append(pltpu.make_async_copy(source.at[part], target.at[part], sem.at[a, c]))
-    for copy in copies:
+            arriving.append(pltpu.make_async_copy(source.at[part], stage.at[part], in_sem.at[a, c]))
+            leaving.append(pltpu.make_async_copy(stage.at[part], target.at[part], out_sem.at[a, c]))
+    for copy in arriving:
         copy.start()
-    for copy in copies:
+    for come, go in zip(arriving, leaving):
+        come.wait()
+        go.start()
+    for copy in leaving:
         copy.wait()
 
 
@@ -377,7 +381,8 @@
         out_shape=tuple(jax.ShapeDtypeStruct(x.shape, x.dtype) for x in found),
         in_specs=[hbm] * 4,
         out_specs=(hbm,) * 4,
-        scratch_shapes=[dma((4, CUTS))],
+        scratch_shapes=[pltpu.VMEM(x.shape, x.dtype) for x in found]
+        + [dma((4, CUTS)), dma((4, CUTS))],
         compiler_params=pltpu.CompilerParams(vmem_limit_bytes=VMEM_BYTES),
         cost_estimate=pl.CostEstimate(flops=0, bytes_accessed=10 * queries.size, transcendentals=0),
     )(*found)

time: 114 us -> 43.9 us (0.39)
  Pallas kernels: 113 us -> 43.1 us
    pallas_call x1, Pallas kernels: 72.7 us -> 2.61 us  [per_device(): pl.pallas_call(hand_over, out_shape=tuple((jax.ShapeDtypeStruct(x.shape,...]
where the time goes in v3:
time: 43.9 us; the launch traced here: 43.7 us
  Pallas kernels  43.1 us (98%)
  between operations  0.64 us (1%)
    pallas_call x1, Pallas kernels, per_device(): pl.pallas_call(functools.partial(kernel, n_ctx, n_grp, spans.shape[0], ti...  40.5 us
    pallas_call x1, Pallas kernels, per_device(): pl.pallas_call(hand_over, out_shape=tuple((jax.ShapeDtypeStruct(x.shape,...  2.61 us

profile of v3, /device:TPU:0, one launch (start us, length us, event | category | flops | bytes accessed | tf_op | source)
XLA Modules:
  0.0 43.7 jit_solution(153893422841731051)
XLA Ops:
  0.6 40.5 %shard_map.93 = (bf16[128,4096]{1,0:T(8,128)(2,1)}, bf16[128,4096]{1,0:T(8,128)(2,1)}, bf16[128,512]{1,0:T(8,128)(2,1)}, bf16[128,512]{1,0:T(8,128)(2,1)}) custom-call(s32[4,3]{1,0:T(4,128)} %spans_hbm.1, f32[1,128]{1,0:T(1,128)} %bitcast.1, bf16[128,4096]{1,0:T(8,128)(2,1)} %q_hbm.1, bf16[128,512]{1,0:T(8,128)(2,1)} %k_hbm.1, bf16[128,512]{1,0:T(8,128)(2,1)} %v_hbm.1, ...), custom_call_target="tpu_custom_call" | custom-call | flops 3221225472 | bytes 4194304 | tf_op jit(solution)/shard_map/pallas_call | solution.py:347
  41.1 2.6 %shard_map.94 = (bf16[128,4096]{1,0:T(8,128)(2,1)}, bf16[128,4096]{1,0:T(8,128)(2,1)}, bf16[128,512]{1,0:T(8,128)(2,1)}, bf16[128,512]{1,0:T(8,128)(2,1)}) custom-call(bf16[128,4096]{1,0:T(8,128)(2,1)} %get-tuple-element.8.refs_0_, bf16[128,4096]{1,0:T(8,128)(2,1)} %get-tuple-element.9.refs_1_, bf16[128,512]{1,0:T(8,128)(2,1)} %get-tuple-element.10.refs_2_, ...), custom_call_target="tpu_custom_call" | custom-call | bytes 5242880 | tf_op jit(solution)/shard_map/pallas_call | solution.py:379

commit v4 on v3

--- a/solution.py
+++ b/solution.py
@@ -58,7 +58,7 @@
     def own_copy(hbm, sem, which, g):
         return pltpu.make_async_copy(
             hbm.at[:, pl.ds(g * HEAD_SIZE, HEAD_SIZE)],
-            kv_buf.at[g, which, pl.ds(0, tile)], sem.at[g])
+            kv_buf.at[g, 0, which], sem.at[g])
 
     def wide_copy(hbm, buf, sem, g):
         return pltpu.make_async_copy(hbm.at[:, pl.ds(g * width, width)], buf.at[g], sem.at[g])
@@ -119,8 +119,7 @@
     for d in range(1, MAX_TILES):
         @pl.when(me < d)
         def _():
-            kv_buf[:, :, d * tile:(d + 1) * tile, :] = jnp.zeros(
-                (KEY_VALUE_HEADS, 2, tile, HEAD_SIZE), BF16)
+            kv_buf[:, d] = jnp.zeros((KEY_VALUE_HEADS, 2, tile, HEAD_SIZE), BF16)
 
         @pl.when(me + d >= n_ctx)
         def _():
@@ -140,12 +139,50 @@
             send_sem=r_send.at[o - 1], recv_sem=r_recv.at[o - 1],
             device_id=(lax.rem(grp + o, n_grp), me), device_id_type=MESH)
 
-    def kv_copy(g, d):
+    place = lax.rem(me, REACH)
+    even, low = lax.rem(place, 2) == 0, place < 2
+    below = me >= REACH
+    relay_from = jnp.where(low, 2 - place, 5 - place)
+    relay_slot = jnp.where(low, 3, 1)
+    relay_step = jnp.where(place == 0, 1, jnp.where(place == 1, 2, jnp.where(place == 2, -2, -1)))
+
+    def kv_send_copy(g, j, source, step, target):
         return pltpu.make_async_remote_copy(
-            src_ref=kv_buf.at[g, :, pl.ds(0, tile)],
-            dst_ref=kv_buf.at[g, :, pl.ds(d * tile, tile)],
-            send_sem=kv_send.at[g, d - 1], recv_sem=kv_recv.at[g, d - 1],
-            device_id=(grp, jnp.minimum(me + d, n_ctx - 1)), device_id_type=MESH)
+            src_ref=kv_buf.at[g, source], dst_ref=kv_buf.at[g, target],
+            send_sem=kv_send.at[g, j], recv_sem=kv_recv.at[g, target - 1],
+            device_id=(grp, lax.rem(me + step + n_ctx, n_ctx)), device_id_type=MESH)
+
+    def kv_plan(g):
+        return (
+            (me + REACH < n_ctx, lambda: kv_send_copy(g, 0, 0, REACH, REACH)),
+            (even, lambda: kv_send_copy(g, 1, 0, 1, 1)),
+            (low, lambda: kv_send_copy(g, 2, 0, 2, 2)),
+            (jnp.logical_and(jnp.logical_not(even), below),
+             lambda: kv_send_copy(g, 1, REACH, -1, 3)),
+            (jnp.logical_and(jnp.logical_not(low), below),
+             lambda: kv_send_copy(g, 2, REACH, -2, 2)),
+            (me >= relay_from, lambda: kv_send_copy(g, 3, relay_from, relay_step, relay_slot)),
+        )
+
+    def kv_arrived(g, slot):
+        kv_send_copy(g, 0, 0, 1, slot).wait_recv()
+
+    def start_some(plan):
+        for condition, copy in plan:
+            @pl.when(condition)
+            def _():
+                copy().start()
+
+    def forward(g):
+        @pl.when(below)
+        def _():
+            kv_arrived(g, REACH)
+        start_some(kv_plan(g)[3:5])
+
+        @pl.when(me >= relay_from)
+        def _():
+            kv_arrived(g, relay_from)
+        start_some(kv_plan(g)[5:])
 
     def grad_copy(g, d):
         return pltpu.make_async_remote_copy(
@@ -164,10 +201,8 @@
     for g in range(KEY_VALUE_HEADS):
         own_copy(k_hbm, k_sem, 0, g).wait()
         own_copy(v_hbm, v_sem, 1, g).wait()
-        for d in range(1, MAX_TILES):
-            @pl.when(me + d < n_ctx)
-            def _():
-                kv_copy(g, d).start()
+        start_some(kv_plan(g)[:3])
+    forward(0)
 
     loop(1, n_ctx, lambda o: margin_copy(o).wait_recv())
     margins = jnp.sum(marg[...], axis=0)
@@ -184,16 +219,20 @@
     def group(g, carry):
         wide_copy(q_hbm, q_buf, q_sem, g).wait()
         wide_copy(du_hbm, du_buf, du_sem, g).wait()
-        for d in range(1, MAX_TILES):
-            @pl.when(me >= d)
-            def _():
-                kv_copy(g, d).wait_recv()
+        @pl.when(g + 1 < KEY_VALUE_HEADS)
+        def _():
+            forward(g + 1)
+
+        for d in range(1, REACH):
+            @pl.when(jnp.logical_and(me >= d, d != relay_from))
+            def _():
+                kv_arrived(g, d)
 
         def merged(which):
-            far = kv_buf[g, which, REACH * tile:(REACH + 1) * tile].astype(F32)
-            parts = [kv_buf[g, which, 0:tile]]
+            far = kv_buf[g, REACH, which].astype(F32)
+            parts = [kv_buf[g, 0, which]]
             for d in range(1, SLOTS):
-                near = kv_buf[g, which, d * tile:(d + 1) * tile].astype(F32)
+                near = kv_buf[g, d, which].astype(F32)
                 parts.append((near * (1.0 - swap[d - 1]) + far * swap[d - 1]).astype(BF16))
             return jnp.concatenate(parts, axis=0)
 
@@ -283,10 +322,13 @@
     lax.fori_loop(0, KEY_VALUE_HEADS, group, 0)
 
     for g in range(KEY_VALUE_HEADS):
+        for condition, copy in kv_plan(g):
+            @pl.when(condition)
+            def _():
+                copy().wait_send()
         for d in range(1, MAX_TILES):
             @pl.when(me + d < n_ctx)
             def _():
-                kv_copy(g, d).wait_send()
                 grad_copy(g, d).wait_recv()
         for which, out in ((0, dk_ref), (1, dv_ref)):
             total = own_grad[g, which]
@@ -360,7 +402,7 @@
             pltpu.VMEM(keys.shape, BF16),
             pltpu.VMEM(values.shape, BF16),
             wide, wide, wide, wide,
-            pltpu.VMEM((KEY_VALUE_HEADS, 2, MAX_TILES * tile, HEAD_SIZE), BF16),
+            pltpu.VMEM((KEY_VALUE_HEADS, MAX_TILES, 2, tile, HEAD_SIZE), BF16),
             slots, slots,
             pltpu.VMEM((KEY_VALUE_HEADS, 2, tile, HEAD_SIZE), F32),
             pltpu.VMEM((n_ctx, 8, 128), F32),

time: 43.9 us -> 51.3 us (1.17)
  Pallas kernels: 43.1 us -> 50.5 us
    pallas_call x1, Pallas kernels: 40.5 us -> 47.9 us  [per_device(): pl.pallas_call(functools.partial(kernel, n_ctx, n_grp, spans.shape[0], ti...]
where the time goes in v4:
time: 51.3 us; the launch traced here: 51.1 us
  Pallas kernels  50.5 us (98%)
  between operations  0.64 us (1%)
    pallas_call x1, Pallas kernels, per_device(): pl.pallas_call(functools.partial(kernel, n_ctx, n_grp, spans.shape[0], ti...  47.9 us
    pallas_call x1, Pallas kernels, per_device(): pl.pallas_call(hand_over, out_shape=tuple((jax.ShapeDtypeStruct(x.shape,...  2.61 us

profile of v4, /device:TPU:0, one launch (start us, length us, event | category | flops | bytes accessed | tf_op | source)
XLA Modules:
  0.0 51.1 jit_solution(440347347057765531)
XLA Ops:
  0.6 47.9 %shard_map.93 = (bf16[128,4096]{1,0:T(8,128)(2,1)}, bf16[128,4096]{1,0:T(8,128)(2,1)}, bf16[128,512]{1,0:T(8,128)(2,1)}, bf16[128,512]{1,0:T(8,128)(2,1)}) custom-call(s32[4,3]{1,0:T(4,128)} %spans_hbm.1, f32[1,128]{1,0:T(1,128)} %bitcast.1, bf16[128,4096]{1,0:T(8,128)(2,1)} %q_hbm.1, bf16[128,512]{1,0:T(8,128)(2,1)} %k_hbm.1, bf16[128,512]{1,0:T(8,128)(2,1)} %v_hbm.1, ...), custom_call_target="tpu_custom_call" | custom-call | flops 3221225472 | bytes 4194304 | tf_op jit(solution)/shard_map/pallas_call | solution.py:389
  48.5 2.6 %shard_map.94 = (bf16[128,4096]{1,0:T(8,128)(2,1)}, bf16[128,4096]{1,0:T(8,128)(2,1)}, bf16[128,512]{1,0:T(8,128)(2,1)}, bf16[128,512]{1,0:T(8,128)(2,1)}) custom-call(bf16[128,4096]{1,0:T(8,128)(2,1)} %get-tuple-element.8.refs_0_, bf16[128,4096]{1,0:T(8,128)(2,1)} %get-tuple-element.9.refs_1_, bf16[128,512]{1,0:T(8,128)(2,1)} %get-tuple-element.10.refs_2_, ...), custom_call_target="tpu_custom_call" | custom-call | bytes 5242880 | tf_op jit(solution)/shard_map/pallas_call | solution.py:421
